TPU v7x, 32 devices: a whole 2x2x4 slice. The times are simulated.
32 devices in a mesh: dev: 32 (over z, y, x, core).
Axes of the slice: x: 2, y: 2, z: 4, core: 2. Of those that a mesh axis runs over, the one named last changes fastest.
Arguments:
- residual: float32 [32, 6, 32, 3072], P('dev'), may hold values from -60 to 60
- direction: float32 [32, 6, 32, 3072], P('dev'), may hold values from -60 to 60
- legendre_scalar: bfloat16 [32, 3072, 128], P('dev'), may hold values from -0.109375 to 0.109375
- legendre_plus: bfloat16 [32, 3072, 128], P('dev'), may hold values from -0.109375 to 0.109375
- legendre_minus: bfloat16 [32, 3072, 128], P('dev'), may hold values from -0.109375 to 0.109375
- prior_inverse: float32 [4, 3072], replicated, as said below
- noise_weight: float32 [128, 2, 3, 4096], P('dev'), may hold values from 0.00025 to 0.0025
- order_ids: int32 [32], replicated, may hold values from 1 to 1535, as said below
- live_blocks: int32 [32, 2], P('dev'), may hold values from 1 to 4
- cycle_assign: int32 [128], replicated, may hold values from 0 to 127, each once
- cycle_length: int32 [128], P('dev'), may hold values from 1024 to 4096, as said below
- cycle_shift: int32 [128], P('dev'), may hold values from 0 to 1
Outputs:
- residual_next: float32 [32, 6, 32, 3072], P('dev')
- direction_next: float32 [32, 6, 32, 3072], P('dev')
- step_length: float32 [32], replicated
Inputs may be any that keep to these rules, and one draw needn't show every extreme that they name: `order_ids`: the values are distinct; each pair holds two different orders below 3072. `cycle_length`: multiples of 4. `cycle_assign`: each latitude pair appears once. `prior_inverse`: for every degree tt and ee are positive, bb is positive and te squared is below tt ee.
All inputs are finite; a program needn't handle non-finite values.
Results may differ from a plain program's by a relative error of at most 0.003.
Values may be sent and summed in bfloat16 or wider, within the bound.
A program may use at most 128 MiB of HBM per device.

v0:
```python
import jax
import jax.numpy as jnp
from jax import lax
from jax.sharding import PartitionSpec as P

L = 3072
BLOCKS = 4


def segment_split(coeffs, order_m):
    degree = jnp.arange(L, dtype=jnp.int32)
    first_seg = degree < L - order_m
    zeros = jnp.zeros_like(coeffs)
    halves = jnp.stack([jnp.where(first_seg, coeffs, zeros), jnp.where(first_seg, zeros, coeffs)])
    return halves.reshape(2, coeffs.shape[0], coeffs.shape[1], L // 2, 2)


def pair_sign(order_m):
    odd_sign = jnp.where(order_m % 2 == 0, 1.0, -1.0).astype(jnp.float32)
    return jnp.stack([jnp.ones((), jnp.float32), odd_sign])


def alive_mask(alive_count, total):
    blocks = jnp.arange(total, dtype=jnp.int32) // (total // BLOCKS)
    return blocks[None, :] < alive_count[:, None]


def spin_forward(part_scalar, part_plus, part_minus, signs):
    signs = signs[:, None, None, None]

    def hemis(part, flip):
        return jnp.stack(
            [part[:, 0] + part[:, 1], flip * signs * (part[:, 0] - part[:, 1])], axis=1
        )

    scalar_h = hemis(part_scalar, 1.0)
    plus_h = hemis(part_plus, 1.0)
    minus_h = hemis(part_minus, -1.0)
    q_real = -(plus_h[:, :, 0] - minus_h[:, :, 3])
    q_imag = -(plus_h[:, :, 1] + minus_h[:, :, 2])
    u_real = -(plus_h[:, :, 2] + minus_h[:, :, 1])
    u_imag = -(plus_h[:, :, 3] - minus_h[:, :, 0])
    return jnp.stack([scalar_h[:, :, 0], scalar_h[:, :, 1], q_real, q_imag, u_real, u_imag], axis=2)


def spin_inputs(grads):
    scalar_in = grads[:, :, 0:2]
    plus_in = jnp.stack(
        [-grads[:, :, 2], -grads[:, :, 3], -grads[:, :, 4], -grads[:, :, 5]], axis=2
    )
    minus_in = jnp.stack([grads[:, :, 5], -grads[:, :, 4], -grads[:, :, 3], grads[:, :, 2]], axis=2)
    return (scalar_in, plus_in, jnp.flip(minus_in, axis=1))


def forward_columns(halves, tables, signs):
    scalar_t, plus_t, minus_t = tables

    def contract(table, rows):
        return jnp.einsum("acsiq,iqk->aqcsk", rows, table, preferred_element_type=jnp.float32)

    return spin_forward(
        contract(scalar_t, halves[:, 0:2]),
        contract(plus_t, halves[:, 2:6]),
        contract(minus_t, halves[:, 2:6]),
        signs,
    )


def adjoint_columns(grads, tables):
    scalar_t, plus_t, minus_t = tables
    scalar_in, plus_in, minus_in = spin_inputs(grads)

    def contract(table, rows):
        return jnp.einsum(
            "iqk,aqcsk->acsiq",
            table,
            rows,
            preferred_element_type=jnp.float32,
            precision=lax.Precision.HIGHEST,
        )

    return jnp.concatenate(
        [contract(scalar_t, scalar_in), contract(plus_t, plus_in) + contract(minus_t, minus_in)],
        axis=1,
    )


def prior_apply(coeffs, prior, order_m):
    first_seg = jnp.arange(L, dtype=jnp.int32) < L - order_m
    doubled = jnp.concatenate([prior, prior], axis=1)
    shifted = lax.dynamic_slice_in_dim(doubled, order_m, L, 1)
    table = jnp.where(first_seg[None, :], shifted, prior)
    temper = coeffs[0:2]
    egrad = coeffs[2:4]
    bmodes = coeffs[4:6]
    return jnp.concatenate(
        [
            table[0] * temper + table[1] * egrad,
            table[1] * temper + table[2] * egrad,
            table[3] * bmodes,
        ],
        axis=0,
    )


def cycle_basis(orders, length, shift, pix):
    pixels = jnp.arange(pix, dtype=jnp.int32)
    turns = orders[:, None] * (2 * pixels[None, :] + shift) % (2 * length)
    angle = turns.astype(jnp.float32) * (jnp.float32(jnp.pi) / length.astype(jnp.float32))
    return jnp.stack([2.0 * jnp.cos(angle), -2.0 * jnp.sin(angle)], axis=1).astype(jnp.bfloat16)


def cycle_slot(field, orders, order_sign, length, shift, weight):
    sims = field.shape[3]
    pix = weight.shape[2]
    basis = cycle_basis(orders, length, shift, pix)
    sky_map = jnp.einsum(
        "mhcrs,mrj->hcsj",
        field.reshape(-1, 2, 3, 2, sims),
        basis,
        preferred_element_type=jnp.float32,
    )
    inside = jnp.arange(pix, dtype=jnp.int32) < length
    weighted = jnp.where(inside, sky_map * weight[:, :, None, :], 0.0).astype(jnp.bfloat16)
    back = jnp.einsum("mrj,hcsj->mhcrs", basis, weighted, preferred_element_type=jnp.float32)
    back = back.reshape(-1, 2, 6, sims)
    signs = order_sign[:, None, None]
    return jnp.stack([back[:, 0] + signs * back[:, 1], back[:, 0] - signs * back[:, 1]], axis=1)


def body(
    residual,
    direction,
    legendre_scalar,
    legendre_plus,
    legendre_minus,
    prior_inverse,
    noise_weight,
    order_ids,
    live_blocks,
    cycle_assign,
    cycle_length,
    cycle_shift,
):
    pairs_here = direction.shape[0]
    sims = direction.shape[2]
    pairs_all = legendre_scalar.shape[2]
    slots = cycle_length.shape[0]
    first = lax.axis_index("dev") * pairs_here
    my_orders = lax.dynamic_slice_in_dim(order_ids, first, pairs_here, 0)
    local_norm = jnp.sum(residual * residual, axis=(0, 1, 3))
    norm_early = lax.psum(local_norm, "dev")
    coeffs = direction.astype(jnp.bfloat16)

    def forward_pair(packed):
        rows, scalar_t, plus_t, minus_t, order_m, alive_count = packed
        halves = segment_split(rows, order_m)
        tables = [table.reshape(L // 2, 2, pairs_all) for table in (scalar_t, plus_t, minus_t)]
        signs = pair_sign(order_m)
        field = forward_columns(halves, tables, signs)
        alive = alive_mask(alive_count, pairs_all)
        return jnp.where(alive[:, None, None, None, :], field, 0.0).astype(jnp.bfloat16)

    fields = lax.map(
        forward_pair,
        (coeffs, legendre_scalar, legendre_plus, legendre_minus, my_orders, live_blocks),
    )
    fields = fields.reshape(2 * pairs_here, 2, 6, sims, pairs_all)
    outgoing = jnp.take(fields, cycle_assign, axis=4)
    all_orders = jnp.stack([order_ids, L - order_ids], axis=1).reshape(-1)
    order_count = all_orders.shape[0]
    order_sign = jnp.where(
        (jnp.arange(order_count, dtype=jnp.int32) % 2 == 0) | (all_orders % 2 == 0), 1.0, -1.0
    ).astype(jnp.float32)
    arrived = lax.all_to_all(outgoing, "dev", split_axis=4, concat_axis=0, tiled=True)
    results = []
    for slot in range(slots):
        results.append(
            cycle_slot(
                arrived[..., slot],
                all_orders,
                order_sign,
                cycle_length[slot],
                cycle_shift[slot],
                noise_weight[slot],
            )
        )
    parity = lax.all_to_all(
        jnp.stack(results, axis=4).astype(jnp.bfloat16),
        "dev",
        split_axis=0,
        concat_axis=4,
        tiled=True,
    ).astype(jnp.float32)
    inverse = (
        jnp.zeros((pairs_all,), jnp.int32)
        .at[cycle_assign]
        .set(jnp.arange(pairs_all, dtype=jnp.int32))
    )
    grads = jnp.take(parity, inverse, axis=4).reshape(pairs_here, 2, 2, 6, sims, pairs_all)

    def adjoint_pair(packed):
        stacked, scalar_t, plus_t, minus_t, order_m, alive_count = packed
        alive = alive_mask(alive_count, pairs_all)
        stacked = jnp.where(alive[:, None, None, None, :], stacked, jnp.zeros_like(stacked))
        tables = [
            table.reshape(L // 2, 2, pairs_all).astype(jnp.float32)
            for table in (scalar_t, plus_t, minus_t)
        ]
        noise = adjoint_columns(stacked, tables)
        noise = noise.reshape(2, 6, sims, L)
        first_seg = jnp.arange(L, dtype=jnp.int32) < L - order_m
        return jnp.where(first_seg, noise[0], noise[1])

    noise_term = lax.map(
        adjoint_pair,
        (grads, legendre_scalar, legendre_plus, legendre_minus, my_orders, live_blocks),
    )
    prior_term = jax.vmap(prior_apply, in_axes=(0, None, 0))(direction, prior_inverse, my_orders)
    image = prior_term + noise_term
    local_curve = jnp.sum(direction * image, axis=(0, 1, 3))
    curvature = lax.psum(local_curve, "dev")
    step_length = norm_early / curvature
    residual_next = residual - step_length[None, None, :, None] * image
    norm_new = lax.psum(jnp.sum(residual_next * residual_next, axis=(0, 1, 3)), "dev")
    direction_next = residual_next + (norm_new / norm_early)[None, None, :, None] * direction
    return (residual_next, direction_next, step_length)


def solution(mesh):
    return jax.shard_map(
        body,
        mesh=mesh,
        in_specs=(
            P("dev", None, None, None),
            P("dev", None, None, None),
            P("dev", None, None),
            P("dev", None, None),
            P("dev", None, None),
            P(),
            P("dev", None, None, None),
            P(),
            P("dev", None),
            P(),
            P("dev"),
            P("dev"),
        ),
        out_specs=(P("dev", None, None, None), P("dev", None, None, None), P()),
        check_vma=False,
    )
```

profile of v0, /device:TPU:0, one launch (start us, length us, event | category | flops | bytes accessed | tf_op | source)
XLA Modules:
  0.0 334.9 jit_solution(8779762617619737354)
XLA Ops:
  9.8 3.3 copy.151
  13.2 10.1 %copy.153 = bf16[1,6,32,1536,2]{3,2,1,0,4:T(8,128)(2,1)S(1)} copy(bf16[1,6,32,1536,2]{2,4,3,1,0:T(2,128)(2,1)} %bitcast.219) | data formatting | bytes 2359296 | tf_op jit(solution)/shard_map/while/body/eval_jaxpr/stack | solution.py:14
  23.2 3.3 copy.152
  26.6 10.1 %copy.154 = bf16[1,6,32,1536,2]{3,2,1,0,4:T(8,128)(2,1)S(1)} copy(bf16[1,6,32,1536,2]{2,4,3,1,0:T(2,128)(2,1)} %bitcast.220) | data formatting | bytes 2359296 | tf_op jit(solution)/shard_map/while/body/eval_jaxpr/stack | solution.py:14
  41.7 2.9 gather_fusion
  46.6 7.3 %all-to-all-start = ((bf16[32,2,1536]{2,1,0:T(2,128)(2,1)}), bf16[32,2,1536]{2,1,0:T(2,128)(2,1)S(1)}, u32[]{:S(2)}, u32[]{:S(2)}) async-start(bf16[32,2,1536]{2,1,0:T(2,128)(2,1)} %reshape.925), calls=%async_computation | async-start | bytes 393216 | tf_op jit(solution)/shard_map/all_to_all | solution.py:175
  69.0 71.4 %multiply_convert_fusion.7 = (bf16[64,1,4096]{2,0,1:T(8,128)(2,1)S(1)}, bf16[64,1,4096]{2,0,1:T(8,128)(2,1)S(1)}, bf16[64,1,4096]{2,0,1:T(8,128)(2,1)}, bf16[64,...) fusion(f32[]{:T(128)S(6)} %div.32, ...), kind=kLoop, calls=%fused_computation.75 | loop fusion | flops 14680064 | bytes 4260132 | tf_op jit(solution)/shard_map/convert.25
  148.3 3.1 fusion.42
  151.4 3.4 %fusion.43 = f32[2,3,32,64,2]{3,2,4,1,0:T(8,128)} fusion(bf16[64,2,3,2,32]{4,0,3,2,1:T(8,128)(2,1)S(1)} %bitcast.234, f32[2,3,4096]{2,1,0:T(4,128)} %copy.167, pred[4096]{0:T(1024)(128)(4,1)S(1)} %copy-done.17, bf16[64,1,4096]{2,0,1:T(8,128)(2,1)} %get-tuple-element.130, bf16[64,1,4096]{2,0,1:T(8,128)(2,1)} %get-tuple-element.131), kind=kOutput, calls=%fused_computation.88 | convolution fusion | flops 407633920 | bytes 1298432 | tf_op jit(solution)/shard_map/mrj,hcsj->mhcrs/dot_general | solution.py:125
  163.0 5.8 %all-to-all-start.1 = ((bf16[32,2,1536]{2,1,0:T(2,128)(2,1)}), bf16[32,2,1536]{2,1,0:T(2,128)(2,1)S(1)}, u32[]{:S(2)}, u32[]{:S(2)}) async-start(bf16[32,2,1536]{2,1,0:T(2,128)(2,1)} %reshape.927), calls=%async_computation.1 | async-start | bytes 393216 | tf_op jit(solution)/shard_map/all_to_all | solution.py:188
  171.5 6.2 %all-to-all-done.1 = bf16[32,2,1536]{2,1,0:T(2,128)(2,1)S(1)} async-done(((bf16[32,2,1536]{2,1,0:T(2,128)(2,1)}), bf16[32,2,1536]{2,1,0:T(2,128)(2,1)S(1)}, u32[]{:S(2)}, u32[]{:S(2)}) %all-to-all-start.1) | async-done | bytes 196640 | tf_op jit(solution)/shard_map/all_to_all | solution.py:188
  183.7 5.3 %gather_fusion.1 = f32[128,2,2,6,32]{4,2,3,1,0:T(2,128)} fusion(f32[2,2,6,32,128]{3,1,4,2,0:T(2,128)} %copy.175, s32[1024]{0:T(1024)S(1)} %pad_clamp_fusion), kind=kCustom, calls=%fused_computation.1 | custom fusion | bytes 786944 | tf_op jit(solution)/shard_map/jit(_take)/gather | solution.py:200
  189.1 2.4 copy.176
  192.3 3.1 convolution_bitcast_fusion.4
  200.9 2.6 pad_maximum_fusion
  203.5 13.1 %copy.180 = f32[1,6,32,1536,2]{2,4,3,1,0:T(2,128)} copy(f32[1,6,32,1536,2]{3,2,1,0,4:T(8,128)} %get-tuple-element.78) | data formatting | bytes 4718592 | tf_op jit(solution)/shard_map/while/body/eval_jaxpr/slice | solution.py:213
  216.5 6.7 %copy.182 = f32[1,6,32,3072]{3,2,1,0:T(8,128)} copy(f32[1,6,32,3072]{2,3,1,0:T(8,128)} %bitcast.217) | data formatting | bytes 4718592 | tf_op jit(solution)/shard_map/while/body/eval_jaxpr/squeeze | solution.py:213
  223.2 13.1 %copy.181 = f32[1,6,32,1536,2]{2,4,3,1,0:T(2,128)} copy(f32[1,6,32,1536,2]{3,2,1,0,4:T(8,128)} %get-tuple-element.77) | data formatting | bytes 4718592 | tf_op jit(solution)/shard_map/while/body/eval_jaxpr/slice | solution.py:213
  236.2 6.7 %copy.183 = f32[1,6,32,3072]{3,2,1,0:T(8,128)} copy(f32[1,6,32,3072]{2,3,1,0:T(8,128)} %bitcast.218) | data formatting | bytes 4718592 | tf_op jit(solution)/shard_map/while/body/eval_jaxpr/squeeze | solution.py:213
  243.0 5.1 %multiply_reduce_fusion.1 = (f32[32]{0:T(128)S(1)}, f32[1,6,32,3072]{3,2,1,0:T(8,128)}) fusion(f32[1,6,32,3072]{3,2,1,0:T(8,128)S(1)} %copy-done.2, f32[1,6,32,3072]{3,2,1,0:T(8,128)} %copy.182, f32[1,6,32,3072]{3,2,1,0:T(8,128)} %copy.183, pred[3072]{0:T(1024)(128)(4,1)S(1)} %iota_compare_fusion.4, f32[1,2,32,3072]{3,2,1,0:T(8,128)} %get-tuple-element.83, ...), kind=kLoop, calls=%fused_computation.35 | loop fusion | flops 3538912 | bytes 11799680 | tf_op jit(solution)/shard_map/reduce_sum | solution.py:221
  248.0 38.8 %all-reduce = (f32[32]{0:T(128)S(1)}, f32[32]{0:T(128)S(1)}) all-reduce(f32[32]{0:T(128)S(1)} %multiply_reduce_fusion.2, f32[32]{0:T(128)S(1)} %get-tuple-element.75), channel_id=1, replica_groups=mesh['dev'=32] {'dev'}, use_global_device_ids=true, to_apply=%region_1.0 | all-reduce | flops 64 | bytes 512 | tf_op jit(solution)/shard_map/psum | solution.py:152
  286.8 4.4 %multiply_reduce_fusion = (f32[32]{0:T(128)S(1)}, f32[1,6,32,3072]{3,2,1,0:T(8,128)}) fusion(f32[1,6,32,3072]{3,2,1,0:T(8,128)} %param.12, f32[1,6,32,3072]{3,2,1,0:T(8,128)} %get-tuple-element.76, f32[32]{0:T(128)S(1)} %div.36), kind=kLoop, calls=%fused_computation.33 | loop fusion | flops 2359264 | bytes 7078144 | tf_op jit(solution)/shard_map/reduce_sum | solution.py:225
  291.3 39.9 %psum.23 = f32[32]{0:T(128)S(1)} all-reduce(f32[32]{0:T(128)S(1)} %get-tuple-element.73), channel_id=1, replica_groups=mesh['dev'=32] {'dev'}, use_global_device_ids=true, to_apply=%region_6.7 | all-reduce | flops 32 | bytes 256 | tf_op jit(solution)/shard_map/psum | solution.py:225
  331.2 3.6 %multiply_add_fusion = f32[1,6,32,3072]{3,2,1,0:T(8,128)} fusion(f32[1,6,32,3072]{3,2,1,0:T(8,128)} %get-tuple-element.74, f32[1,6,32,3072]{3,2,1,0:T(8,128)S(1)} %copy-done.2, f32[32]{0:T(128)S(1)} %div.37), kind=kLoop, calls=%fused_computation.32 | loop fusion | flops 1179648 | bytes 7078016 | tf_op jit(solution)/shard_map/add | solution.py:226
  (137 shorter events, 51.7 us)
Async XLA Ops:
  0.6 36.0 %copy-start = (bf16[1,3072,128]{2,1,0:T(8,128)(2,1)S(1)}, bf16[1,3072,128]{2,1,0:T(8,128)(2,1)}, u32[]{:S(2)}) copy-start(bf16[1,3072,128]{2,1,0:T(8,128)(2,1)} %param.15) | copy-start | bytes 2359300
  41.0 5.6 %copy-start.21 = (pred[2,128]{1,0:T(4,128)(4,1)}, pred[2,128]{1,0:T(4,128)(4,1)S(1)}, u32[]{:S(2)}) copy-start(pred[2,128]{1,0:T(4,128)(4,1)S(1)} %broadcast_compare_fusion) | copy-start | bytes 772
  41.0 12.9 %copy-start.15 = (s32[4]{0:T(128)S(1)}, s32[4]{0:T(128)}, u32[]{:S(2)}) copy-start(s32[4]{0:T(128)} %param.22) | copy-start | bytes 52
  41.0 18.4 %copy-start.26 = (s32[32]{0:T(128)S(1)}, s32[32]{0:T(128)}, u32[]{:S(2)}) copy-start(s32[32]{0:T(128)} %param.19) | copy-start | bytes 388
  41.0 20.8 %copy-start.16 = (s32[4]{0:T(128)S(1)}, s32[4]{0:T(128)}, u32[]{:S(2)}) copy-start(s32[4]{0:T(128)} %param.23) | copy-start | bytes 52
  41.0 21.9 %copy-start.11 = (f32[4,2,3,4096]{3,1,2,0:T(2,128)S(1)}, f32[4,2,3,4096]{3,1,2,0:T(2,128)}, u32[]{:S(2)}) copy-start(f32[4,2,3,4096]{3,1,2,0:T(2,128)} %param.18) | copy-start | bytes 1179652
  41.6 23.9 %copy-start.14 = (f32[4,3072]{1,0:T(4,128)S(1)}, f32[4,3072]{1,0:T(4,128)}, u32[]{:S(2)}) copy-start(f32[4,3072]{1,0:T(4,128)} %param.17) | copy-start | bytes 147460
  46.6 99.5 %all-to-all-start = ((bf16[32,2,1536]{2,1,0:T(2,128)(2,1)}), bf16[32,2,1536]{2,1,0:T(2,128)(2,1)S(1)}, u32[]{:S(2)}, u32[]{:S(2)}) async-start(bf16[32,2,1536]{2,1,0:T(2,128)(2,1)} %reshape.925), calls=%async_computation | async-start | bytes 393216 | tf_op jit(solution)/shard_map/all_to_all | solution.py:175
  148.3 3.1 copy-start.17
  151.4 3.4 %copy-start.9 = (bf16[64,1,4096]{2,0,1:T(8,128)(2,1)S(1)}, bf16[64,1,4096]{2,0,1:T(8,128)(2,1)}, u32[]{:S(2)}) copy-start(bf16[64,1,4096]{2,0,1:T(8,128)(2,1)} %get-tuple-element.133) | copy-start | bytes 1572868
  151.4 3.4 %copy-start.19 = (pred[4096]{0:T(1024)(128)(4,1)S(1)}, pred[4096]{0:T(1024)(128)(4,1)}, u32[]{:S(2)}) copy-start(pred[4096]{0:T(1024)(128)(4,1)} %iota_compare_fusion.2) | copy-start | bytes 12292
  156.9 2.1 copy-start.12
  156.9 2.1 copy-start.13
  156.9 2.1 copy-start.24
  159.1 9.7 %copy-start.2 = (f32[1,6,32,3072]{3,2,1,0:T(8,128)S(1)}, f32[1,6,32,3072]{3,2,1,0:T(8,128)}, u32[]{:S(2)}) copy-start(f32[1,6,32,3072]{3,2,1,0:T(8,128)} %param.13) | copy-start | bytes 7077892
  163.0 14.7 %all-to-all-start.1 = ((bf16[32,2,1536]{2,1,0:T(2,128)(2,1)}), bf16[32,2,1536]{2,1,0:T(2,128)(2,1)S(1)}, u32[]{:S(2)}, u32[]{:S(2)}) async-start(bf16[32,2,1536]{2,1,0:T(2,128)(2,1)} %reshape.927), calls=%async_computation.1 | async-start | bytes 393216 | tf_op jit(solution)/shard_map/all_to_all | solution.py:188
  168.8 2.4 copy-start.25
  168.8 2.4 copy-start.3
  181.4 10.2 %copy-start.22 = (pred[2,128]{1,0:T(4,128)(4,1)S(1)}, pred[2,128]{1,0:T(4,128)(4,1)}, u32[]{:S(2)}) copy-start(pred[2,128]{1,0:T(4,128)(4,1)} %copy-done.21) | copy-start | bytes 772
  181.4 10.2 %copy-start.23 = (pred[128]{0:T(512)(128)(4,1)S(1)}, pred[128]{0:T(512)(128)(4,1)}, u32[]{:S(2)}) copy-start(pred[128]{0:T(512)(128)(4,1)} %get-tuple-element.147) | copy-start | bytes 388
  197.0 2.4 copy-start.8
  236.2 6.7 %copy-start.6 = (f32[1,2,32,3072]{3,2,1,0:T(8,128)S(1)}, f32[1,2,32,3072]{3,2,1,0:T(8,128)}, u32[]{:S(2)}) copy-start(f32[1,2,32,3072]{3,2,1,0:T(8,128)} %get-tuple-element.79) | copy-start | bytes 2359300
  286.8 4.4 %copy-start.27 = (f32[32]{0:T(128)}, f32[32]{0:T(128)S(1)}, u32[]{:S(2)}) copy-start(f32[32]{0:T(128)S(1)} %div.36) | copy-start | bytes 388
  331.2 3.6 %copy-start.1 = (bf16[1,3072,128]{2,1,0:T(8,128)(2,1)S(1)}, bf16[1,3072,128]{2,1,0:T(8,128)(2,1)}, u32[]{:S(2)}) copy-start(bf16[1,3072,128]{2,1,0:T(8,128)(2,1)} %param.15) | copy-start | bytes 2359300
  (8 other events, 12.1 us)
where the time goes:
time: 336 us; the launch traced here: 335 us
  other arithmetic  106 us (32%)
  local copies, waits for them, and re-layouts  99.5 us (30%)
  blocking collectives  78.7 us (23%)
  matrix products  19.7 us (6%)
  starting transfers between devices  13.1 us (4%)
  between operations  11.7 us (3%)
  waiting for transfers between devices  6.19 us (2%)
    another operation x2, other arithmetic  71.5 us
    psum x1, blocking collectives, body(): lax.psum(jnp.sum(residual_next * residual_next, axis=(0, 1, 3)), 'dev')  39.9 us
    psum x1, blocking collectives, body(): norm_early = lax.psum(local_norm, 'dev')  38.8 us
    slice x2, local copies, waits for them, and re-layouts, adjoint_pair(): return jnp.where(first_seg, noise[0], noise[1])  26.1 us
    another operation x2, local copies, waits for them, and re-layouts, segment_split(): jnp.stack([jnp.where(first_seg, coeffs, zeros), jnp.where(first_seg, zero...  20.1 us
    squeeze x2, local copies, waits for them, and re-layouts, adjoint_pair(): return jnp.where(first_seg, noise[0], noise[1])  13.4 us
    dot_general x4, matrix products, cycle_slot(): jnp.einsum('mrj,hcsj->mhcrs', basis, weighted, preferred_element_type=jnp...  10.6 us
    gather x2, local copies, waits for them, and re-layouts, body(): jnp.take(parity, inverse, axis=4)  7.78 us
  transfers between devices with their start and end apart: 2, of which 1 were waited for; matrix products, arithmetic and copies ran while one was open for 26% of the time, Pallas kernels for 0%

commit v1 on v0

v1 whole, which is shorter than its diff:
```python
import functools

import jax
import jax.numpy as jnp
from jax import lax
from jax.experimental import pallas as pl
from jax.experimental.pallas import tpu as pltpu
from jax.sharding import PartitionSpec as P

L = 3072
BLOCKS = 4
JC = 512
PC = 512
F32 = jnp.float32
BF16 = jnp.bfloat16
NT = (((1,), (1,)), ((), ()))
MESH = pl.DeviceIdType.MESH


def dot(a, b):
    return jnp.dot(a, b, preferred_element_type=F32)


def dot_nt(a, b):
    return lax.dot_general(a, b, NT, preferred_element_type=F32)


def iota(shape, axis):
    return lax.broadcasted_iota(jnp.int32, shape, axis)


def turn(count, length):
    whole = 2 * length
    inv = 1.0 / whole.astype(F32)
    quot = jnp.floor(count.astype(F32) * inv).astype(jnp.int32)
    rest = count - quot * whole
    rest = jnp.where(rest < 0, rest + whole, rest)
    rest = jnp.where(rest >= whole, rest - whole, rest)
    t = (rest - length).astype(F32) * inv * F32(jnp.pi)
    t2 = t * t
    s = 1.0 / 6227020800.0
    for c in (-1.0 / 39916800, 1.0 / 362880, -1.0 / 5040, 1.0 / 120, -1.0 / 6, 1.0):
        s = s * t2 + c
    s = s * t
    k = 1.0 / 479001600.0
    for c in (-1.0 / 3628800, 1.0 / 40320, -1.0 / 720, 1.0 / 24, -0.5, 1.0):
        k = k * t2 + c
    return 2.0 * s * s - 1.0, -2.0 * s * k


def kernel(
    nd, slots, K, sims, pix,
    res_h, dir_h, ts_h, tp_h, tm_h, nw_h, prior_ref, ids_ref, assign_ref,
    ids_s, live_s, len_s, shift_s,
    image_h, stats_ref,
    res, drn, ts, teb, nw, E, acc_t, acc_eb, F, send1, recv1, send2, recv2,
    basis, weighted, PAR, lt, leb, prior, image, accs, psend, precv,
    in_sem, s1, r1, s2, r2, s3, r3, own_sem, out_sem,
):
    me = lax.axis_index("dev")
    rows = 4 * slots
    total_rows = rows * nd
    order_rows = 2 * nd
    cs = 3 * sims

    loads = [
        pltpu.make_async_copy(dir_h.at[0], drn, in_sem.at[0]),
        pltpu.make_async_copy(ts_h.at[0], ts, in_sem.at[1]),
        pltpu.make_async_copy(tp_h.at[0], teb.at[:, pl.ds(0, K)], in_sem.at[2]),
        pltpu.make_async_copy(tm_h.at[0], teb.at[:, pl.ds(K, K)], in_sem.at[3]),
        pltpu.make_async_copy(nw_h, nw, in_sem.at[4]),
        pltpu.make_async_copy(res_h.at[0], res, in_sem.at[5]),
    ]
    for load in loads:
        load.start()

    barrier = pltpu.get_barrier_semaphore()

    def greet(i, carry):
        pl.semaphore_signal(
            barrier, inc=1, device_id=(lax.rem(me + i, nd),), device_id_type=MESH
        )
        return carry

    lax.fori_loop(1, nd, greet, 0)

    my_m = ids_s[me]
    odd_sign = jnp.where(lax.rem(my_m, 2) == 0, F32(1.0), F32(-1.0))

    onehot_t = (iota((K, K), 0) == assign_ref[...]).astype(F32).astype(BF16)

    def build_e(c, carry):
        r0 = c * 128
        row = iota((128, K), 0) + r0
        pick = (row // 4 == iota((128, K), 1)).astype(F32).astype(BF16)
        block = dot_nt(pick, onehot_t)
        for oh in range(4):
            E[pl.ds(pl.multiple_of(r0, 128), 128), oh * K : (oh + 1) * K] = jnp.where(
                row % 4 == oh, block, 0.0
            ).astype(BF16)
        return carry

    lax.fori_loop(0, total_rows // 128, build_e, 0)

    for load in loads[:4]:
        load.wait()

    def lane_masks(j0):
        lane = iota((1, JC), 1) + j0
        return lane < L - my_m, lane % 2 == 0

    for c in range(L // JC):
        first, even = lane_masks(c * JC)
        alt = jnp.where(even, 1.0, -1.0)
        m0 = first.astype(F32)
        m1 = 1.0 - m0
        x = drn[:, :, c * JC : (c + 1) * JC].reshape(6 * sims, JC)
        parts = [(x * m).astype(BF16) for m in (m0, m0 * alt, m1, m1 * alt)]
        lhs_t = jnp.concatenate([p[: 2 * sims] for p in parts], axis=0)
        lhs_eb = jnp.concatenate([p[2 * sims :] for p in parts], axis=0)
        add_t = dot(lhs_t, ts[c * JC : (c + 1) * JC, :])
        add_eb = dot(lhs_eb, teb[c * JC : (c + 1) * JC, :])
        if c == 0:
            acc_t[...] = add_t
            acc_eb[...] = add_eb
        else:
            acc_t[...] += add_t
            acc_eb[...] += add_eb

    def alive(s, height):
        return iota((height, K), 1) // (K // BLOCKS) < live_s[0, s]

    for s in range(2):
        g = F32(1.0) if s == 0 else odd_sign
        live = alive(s, sims)
        for h in range(2):
            a = 2 * s + h
            sg = F32(1.0) if h == 0 else g
            sx = F32(1.0) if h == 0 else -g
            t0 = 2 * sims * a
            e0 = 4 * sims * a
            t_re = sg * acc_t[t0 : t0 + sims, :]
            t_im = sg * acc_t[t0 + sims : t0 + 2 * sims, :]
            w = [sg * acc_eb[e0 + i * sims : e0 + (i + 1) * sims, 0:K] for i in range(4)]
            v = [sx * acc_eb[e0 + i * sims : e0 + (i + 1) * sims, K : 2 * K] for i in range(4)]
            zero = jnp.zeros((sims, K), F32)
            blocks = [
                t_re, v[3] - w[0], -(w[2] + v[1]), zero,
                t_im, -(w[1] + v[2]), v[0] - w[3], zero,
            ]
            for i, block in enumerate(blocks):
                F[i * sims : (i + 1) * sims, a * K : (a + 1) * K] = jnp.where(
                    live, block, 0.0
                ).astype(BF16)

    CH = min(512, total_rows)

    def fill1(c, carry):
        at = pl.ds(pl.multiple_of(c * CH, CH), CH)
        send1[at, :] = dot_nt(E[at, :], F[...]).astype(BF16)
        return carry

    lax.fori_loop(0, total_rows // CH, fill1, 0)

    pl.semaphore_wait(barrier, nd - 1)

    def block_at(ref, d, size):
        return ref.at[pl.ds(pl.multiple_of(d * size, size), size)]

    def remote(send, recv, ss, rs, i, size):
        dst = lax.rem(me + i, nd)
        return pltpu.make_async_remote_copy(
            src_ref=send if size is None else block_at(send, dst, size),
            dst_ref=recv.at[me] if size is None else block_at(recv, me, size),
            send_sem=ss.at[i],
            recv_sem=rs.at[i],
            device_id=(dst,),
            device_id_type=MESH,
        )

    def start_all(*args):
        def go(i, carry):
            remote(*args[:4], i, args[4]).start()
            return carry

        lax.fori_loop(1, nd, go, 0)

    def wait_recv_all(*args):
        def go(i, carry):
            remote(*args[:4], i, args[4]).wait_recv()
            return carry

        lax.fori_loop(1, nd, go, 0)

    def wait_send_all(*args):
        def go(i, carry):
            remote(*args[:4], i, args[4]).wait_send()
            return carry

        lax.fori_loop(1, nd, go, 0)

    def own(send, recv, i):
        return pltpu.make_async_copy(
            block_at(send, me, rows), block_at(recv, me, rows), own_sem.at[i]
        )

    ex1 = (send1, recv1, s1, r1, rows)
    start_all(*ex1)
    own(send1, recv1, 0).start()

    ids = ids_ref[...].astype(F32)
    OB = min(64, order_rows)
    for ob in range(order_rows // OB):
        row = iota((OB, nd), 0) + ob * OB
        m_col = jnp.sum(
            jnp.where(iota((OB, nd), 1) == row // 2, ids, 0.0), axis=1, keepdims=True
        ).astype(jnp.int32)
        m_full = jnp.broadcast_to(m_col, (OB, 128))
        m_full = jnp.where(iota((OB, 128), 0) % 2 == 0, m_full, L - m_full)
        for tl in range(slots):
            n_full = jnp.full((OB, 128), len_s[tl], jnp.int32)
            spot = 2 * iota((OB, 128), 1) + shift_s[tl]
            co, si = turn(m_full * spot, n_full)
            wc, ws = turn(m_full * 256, n_full)

            def step(a, carry, tl=tl, ob=ob, wc=wc, ws=ws):
                re, im = carry
                at = pl.ds(pl.multiple_of(a * 128, 128), 128)
                basis[tl, ob * OB : (ob + 1) * OB, at] = re.astype(BF16)
                basis[tl, order_rows + ob * OB : order_rows + (ob + 1) * OB, at] = im.astype(BF16)
                return re * wc + im * ws, im * wc - re * ws

            lax.fori_loop(0, pix // 128, step, (2.0 * co, -2.0 * si))

    lane = iota((1, 2 * order_rows), 1)
    spread = (iota((nd, 2 * order_rows), 0) == (lane % order_rows) // 2).astype(F32)
    odd = dot(jnp.broadcast_to((ids_ref[...] % 2).astype(F32), (8, nd)), spread)[0:1]
    g_row = jnp.where((odd > 0.5) & (lane % 2 == 1), -1.0, 1.0)

    pr = prior_ref[...]
    sigma = jnp.maximum(jnp.max(jnp.abs(pr)), 1.0)
    pr8 = jnp.concatenate([pr, pr], axis=0)
    rolled = pltpu.roll(pr8, L - my_m, 1)
    first_row = iota((8, L), 1) < L - my_m
    prior[...] = jnp.where(first_row, rolled, pr8)
    inv_sigma = 1.0 / jnp.full((sims, 128), sigma, F32)

    loads[4].wait()
    loads[5].wait()

    def fold(x):
        x = x[0] + x[1] + x[2] + x[3] + x[4] + x[5]
        out = x[:, 0:128]
        for i in range(1, x.shape[1] // 128):
            out = out + x[:, i * 128 : (i + 1) * 128]
        return out

    norm = jnp.zeros((sims, 128), F32)
    for c in range(L // JC):
        x = res[:, :, c * JC : (c + 1) * JC]
        norm = norm + fold(x * x)
    accs[0:sims, :] = norm
    accs[sims : 4 * sims, :] = jnp.zeros((3 * sims, 128), F32)

    own(send1, recv1, 0).wait()
    wait_recv_all(*ex1)

    def slot(tl, carry):
        a = iota((2 * order_rows, total_rows), 0)
        want = ((a // 2) % nd) * rows + tl * 4 + (a % 2) * 2 + a // order_rows
        sel = (iota((2 * order_rows, total_rows), 1) == want).astype(F32).astype(BF16)
        D = dot(sel, recv1[...])
        mt = jnp.concatenate(
            [
                jnp.concatenate([D[0:order_rows, 0:128], D[order_rows:, 0:128]], axis=1),
                jnp.concatenate([D[0:order_rows, 128:256], D[order_rows:, 128:256]], axis=1),
            ],
            axis=0,
        )
        mm = mt.T
        M = jnp.concatenate([mm[0:cs], mm[128 : 128 + cs]], axis=0).astype(BF16)
        n = len_s[tl]
        for c in range(pix // PC):
            at = slice(c * PC, (c + 1) * PC)
            sky = dot(M, basis[tl, :, at]).reshape(2, 3, sims, PC)
            inside = iota((2, 3, PC), 2) + c * PC < n
            wt = jnp.where(inside, nw[tl, :, :, at], 0.0)
            weighted[:, at] = (sky * wt[:, :, None, :]).reshape(2 * cs, PC).astype(BF16)
        back = dot_nt(weighted[...], basis[tl])
        north = back[0:cs]
        south = back[cs : 2 * cs] * g_row
        pad = jnp.zeros((128 - cs, 2 * order_rows), F32)
        for q, par in enumerate((north + south, north - south)):
            pt = jnp.concatenate([par, pad], axis=0).T.astype(BF16)
            at = pl.ds(pl.multiple_of((tl * 2 + q) * order_rows, order_rows), order_rows)
            PAR[at, 0:128] = pt[0:order_rows]
            PAR[at, 128:256] = pt[order_rows:]
        return carry

    lax.fori_loop(0, slots, slot, 0)

    def fill2(c, carry):
        at = pl.ds(pl.multiple_of(c * CH, CH), CH)
        b = iota((CH, total_rows), 0) + c * CH
        want = ((((b // 4) % slots) * 2 + b % 2) * nd + b // rows) * 2 + (b // 2) % 2
        sel = (iota((CH, total_rows), 1) == want).astype(F32).astype(BF16)
        send2[at, :] = dot(sel, PAR[...]).astype(BF16)
        return carry

    lax.fori_loop(0, total_rows // CH, fill2, 0)

    ex2 = (send2, recv2, s2, r2, rows)
    start_all(*ex2)
    own(send2, recv2, 1).start()
    wait_send_all(*ex1)
    own(send2, recv2, 1).wait()
    wait_recv_all(*ex2)

    GT = dot(recv2[...].astype(F32).T.astype(BF16), E[...])
    for s in range(2):
        live = alive(s, 256)
        G = [
            jnp.where(live, GT[:, (2 * s + q) * K : (2 * s + q + 1) * K], 0.0) for q in range(2)
        ]
        for q in range(2):
            a = 2 * s + q
            A, B = G[q], G[1 - q]
            lt[2 * sims * a : 2 * sims * a + sims, :] = A[0:sims].astype(BF16)
            lt[2 * sims * a + sims : 2 * sims * (a + 1), :] = A[128 : 128 + sims].astype(BF16)
            qr, ur = slice(sims, 2 * sims), slice(2 * sims, 3 * sims)
            qi, ui = slice(128 + sims, 128 + 2 * sims), slice(128 + 2 * sims, 128 + 3 * sims)
            plus = (-A[qr], -A[qi], -A[ur], -A[ui])
            minus = (B[ui], -B[ur], -B[qi], B[qr])
            for i in range(4):
                e0 = 4 * sims * a + i * sims
                leb[e0 : e0 + sims, 0:K] = plus[i].astype(BF16)
                leb[e0 : e0 + sims, K : 2 * K] = minus[i].astype(BF16)

    outs = []
    for c in range(L // JC):
        at = slice(c * JC, (c + 1) * JC)
        first, even = lane_masks(c * JC)
        nt = dot_nt(lt[...], ts[at, :])
        ne = dot_nt(leb[...], teb[at, :])

        def choose(x, size):
            x = [x[i * size : (i + 1) * size] for i in range(4)]
            return jnp.where(
                first, jnp.where(even, x[0], x[1]), jnp.where(even, x[2], x[3])
            )

        nt = choose(nt, 2 * sims).reshape(2, sims, JC)
        ne = choose(ne, 4 * sims).reshape(4, sims, JC)
        tt, te, ee, bb = [prior[i : i + 1, at][None] for i in range(4)]
        d = drn[:, :, at]
        img = jnp.concatenate(
            [
                nt + tt * d[0:2] + te * d[2:4],
                ne[0:2] + te * d[0:2] + ee * d[2:4],
                ne[2:4] + bb * d[4:6],
            ],
            axis=0,
        )
        image[:, :, at] = img
        out = pltpu.make_async_copy(image.at[:, :, at], image_h.at[0, :, :, at], out_sem.at[c])
        out.start()
        outs.append(out)
        scaled = img * inv_sigma[0:1, 0:1][None]
        accs[sims : 2 * sims, :] += fold(d * scaled)
        accs[2 * sims : 3 * sims, :] += fold(res[:, :, at] * scaled)
        accs[3 * sims : 4 * sims, :] += fold(scaled * scaled)

    local = jnp.sum(accs[...].T, axis=0, keepdims=True)
    psend[...] = jnp.broadcast_to(local, (8, 4 * sims))
    precv[me] = psend[...]
    ex3 = (psend, precv, s3, r3, None)
    start_all(*ex3)
    for out in outs:
        out.wait()
    wait_send_all(*ex2)
    wait_recv_all(*ex3)
    total = precv[0]
    for i in range(1, nd):
        total = total + precv[i]
    stats_ref[0:8, :] = total
    stats_ref[8:16, :] = jnp.full((8, 4 * sims), sigma, F32)
    wait_send_all(*ex3)


def body(
    residual, direction, legendre_scalar, legendre_plus, legendre_minus, prior_inverse,
    noise_weight, order_ids, live_blocks, cycle_assign, cycle_length, cycle_shift, nd,
):
    sims = direction.shape[2]
    K = legendre_scalar.shape[2]
    slots = cycle_length.shape[0]
    pix = noise_weight.shape[3]
    assert direction.shape[0] == 1
    rows = 4 * slots
    total_rows = rows * nd
    vmem = pl.BlockSpec(memory_space=pltpu.VMEM)
    smem = pl.BlockSpec(memory_space=pltpu.SMEM)
    hbm = pl.BlockSpec(memory_space=pl.ANY)
    dma = pltpu.SemaphoreType.DMA
    image, stats = pl.pallas_call(
        functools.partial(kernel, nd, slots, K, sims, pix),
        out_shape=(
            jax.ShapeDtypeStruct(direction.shape, F32),
            jax.ShapeDtypeStruct((16, 4 * sims), F32),
        ),
        in_specs=[hbm] * 6 + [vmem] * 3 + [smem] * 4,
        out_specs=(hbm, vmem),
        scratch_shapes=[
            pltpu.VMEM((6, sims, L), F32),
            pltpu.VMEM((6, sims, L), F32),
            pltpu.VMEM((L, K), BF16),
            pltpu.VMEM((L, 2 * K), BF16),
            pltpu.VMEM((slots, 2, 3, pix), F32),
            pltpu.VMEM((total_rows, 4 * K), BF16),
            pltpu.VMEM((8 * sims, K), F32),
            pltpu.VMEM((16 * sims, 2 * K), F32),
            pltpu.VMEM((256, 4 * K), BF16),
            pltpu.VMEM((total_rows, 256), BF16),
            pltpu.VMEM((total_rows, 256), BF16),
            pltpu.VMEM((total_rows, 256), BF16),
            pltpu.VMEM((total_rows, 256), BF16),
            pltpu.VMEM((slots, 4 * nd, pix), BF16),
            pltpu.VMEM((6 * sims, pix), BF16),
            pltpu.VMEM((total_rows, 256), BF16),
            pltpu.VMEM((8 * sims, K), BF16),
            pltpu.VMEM((16 * sims, 2 * K), BF16),
            pltpu.VMEM((8, L), F32),
            pltpu.VMEM((6, sims, L), F32),
            pltpu.VMEM((4 * sims, 128), F32),
            pltpu.VMEM((8, 4 * sims), F32),
            pltpu.VMEM((nd, 8, 4 * sims), F32),
            dma((6,)), dma((nd,)), dma((nd,)), dma((nd,)), dma((nd,)), dma((nd,)), dma((nd,)),
            dma((2,)), dma((L // JC,)),
        ],
        compiler_params=pltpu.CompilerParams(
            collective_id=0, has_side_effects=True, vmem_limit_bytes=60 * 1024 * 1024
        ),
        name="cg",
    )(
        residual, direction, legendre_scalar, legendre_plus, legendre_minus, noise_weight,
        prior_inverse, order_ids.reshape(1, -1), cycle_assign.reshape(1, -1),
        order_ids, live_blocks, cycle_length, cycle_shift,
    )
    norm_old, da, ra, aa = [stats[0, i * sims : (i + 1) * sims] for i in range(4)]
    scaled_step = norm_old / da
    step_length = scaled_step / stats[8, 0:sims]
    norm_new = norm_old - 2.0 * scaled_step * ra + scaled_step * scaled_step * aa
    ratio = norm_new / norm_old
    residual_next = residual - step_length[None, None, :, None] * image
    direction_next = residual_next + ratio[None, None, :, None] * direction
    return (residual_next, direction_next, step_length)


def solution(mesh):
    return jax.shard_map(
        functools.partial(body, nd=mesh.shape["dev"]),
        mesh=mesh,
        in_specs=(
            P("dev", None, None, None),
            P("dev", None, None, None),
            P("dev", None, None),
            P("dev", None, None),
            P("dev", None, None),
            P(),
            P("dev", None, None, None),
            P(),
            P("dev", None),
            P(),
            P("dev"),
            P("dev"),
        ),
        out_specs=(P("dev", None, None, None), P("dev", None, None, None), P()),
        check_vma=False,
    )
```

time: 336 us -> 50.6 us (0.15)
  other arithmetic: 106 us -> 6.54 us
  local copies, waits for them, and re-layouts: 99.5 us -> 2.07 us
  blocking collectives: 78.7 us -> 0 us
  Pallas kernels: 0 us -> 41.1 us
  matrix products: 19.7 us -> 0 us
  starting transfers between devices: 13.1 us -> 0 us
  between operations: 11.7 us -> 0.65 us
  waiting for transfers between devices: 6.19 us -> 0 us
    psum x2 -> x0, blocking collectives: 78.7 us -> none  [the longest x1 39.9 us: body(): lax.psum(jnp.sum(residual_next * residual_next, axis=(0, 1, 3)), 'dev')]
    another operation x12 -> x0, other arithmetic: 72.5 us -> none
    pallas_call x0 -> x1, Pallas kernels: none -> 41.1 us  [body(): pl.pallas_call(functools.partial(kernel, nd, slots, K, sims, pix), out_sh...]
    slice x6 -> x0, local copies, waits for them, and re-layouts: 28.8 us -> none  [the longest x2 26.1 us: adjoint_pair(): return jnp.where(first_seg, noise[0], noise[1])]
    another operation x4 -> x0, local copies, waits for them, and re-layouts: 21.5 us -> none  [the longest x2 20.1 us: segment_split(): jnp.stack([jnp.where(first_seg, coeffs, zeros), jnp.where(first_seg, zero...]
    dot_general x10 -> x0, matrix products: 19.7 us -> none  [the longest x4 10.6 us: cycle_slot(): jnp.einsum('mrj,hcsj->mhcrs', basis, weighted, preferred_element_type=jnp...]
    squeeze x2 -> x0, local copies, waits for them, and re-layouts: 13.4 us -> none  [adjoint_pair(): return jnp.where(first_seg, noise[0], noise[1])]
    all_to_all x2 -> x0, starting transfers between devices: 13.1 us -> none  [the longest x1 7.31 us: body(): lax.all_to_all(outgoing, 'dev', split_axis=4, concat_axis=0, tiled=True)]
  transfers between devices with their start and end apart: 2 -> 0, of which waited for: 1 -> 0; matrix products, arithmetic and copies ran while one was open for 26% -> 0% of each run, Pallas kernels for 0% -> 0%
where the time goes in v1:
time: 50.6 us; the launch traced here: 50.4 us
  Pallas kernels  41.1 us (81%)
  other arithmetic  6.54 us (13%)
  local copies, waits for them, and re-layouts  2.07 us (4%)
  between operations  0.65 us (1%)
    pallas_call x1, Pallas kernels, body(): pl.pallas_call(functools.partial(kernel, nd, slots, K, sims, pix), out_sh...  41.1 us
    add x1, other arithmetic, body(): direction_next = residual_next + ratio[None, None, :, None] * direction  5.63 us
    unnamed x5, local copies, waits for them, and re-layouts  2.07 us

profile of v1, /device:TPU:0, one launch (start us, length us, event | category | flops | bytes accessed | tf_op | source)
XLA Modules:
  0.0 50.4 jit_solution(3810519045539049595)
XLA Ops:
  0.6 2.1 %copy.15.nw_h = f32[4,2,3,4096]{3,2,1,0:T(4,128)} copy(f32[4,2,3,4096]{3,1,2,0:T(2,128)} %param.18) | data formatting | bytes 786432 | tf_op args[6]
  2.7 0.0 copy-start
  2.7 41.1 %cg.1 = (f32[1,6,32,3072]{3,2,1,0:T(8,128)}, f32[16,128]{1,0:T(8,128)}) custom-call(f32[1,6,32,3072]{3,2,1,0:T(8,128)} %res_h.1, f32[1,6,32,3072]{3,2,1,0:T(8,128)} %dir_h.1, bf16[1,3072,128]{2,1,0:T(8,128)(2,1)} %ts_h.1, bf16[1,3072,128]{2,1,0:T(8,128)(2,1)} %tp_h.1, bf16[1,3072,128]{2,1,0:T(8,128)(2,1)} %tm_h.1, f32[4,2,3,4096]{3,2,1,0:T(4,128)} %copy.15.nw_h, ...), custom_call_target="tpu_custom_call" | custom-call | tf_op jit(solution)/shard_map/cg/pallas_call | solution.py:405
  43.8 0.9 %fusion.3 = (f32[32]{0:T(128)S(1)}, f32[32]{0:T(128)S(1)}) fusion(f32[16,128]{1,0:T(8,128)} %get-tuple-element.5), kind=kLoop, calls=%fused_computation.8 | loop fusion | flops 320 | bytes 896 | tf_op jit(solution)/shard_map/div | solution.py:451
  44.7 0.0 copy-start.1
  44.7 0.0 copy-done
  44.7 5.6 %multiply_add_fusion = (f32[1,6,32,3072]{3,2,1,0:T(8,128)}, f32[1,6,32,3072]{3,2,1,0:T(8,128)}) fusion(f32[1,6,32,3072]{3,2,1,0:T(8,128)S(1)} %copy-done, f32[32]{0:T(128)S(1)} %get-tuple-element.10, f32[1,6,32,3072]{3,2,1,0:T(8,128)} %res_h.1, f32[1,6,32,3072]{3,2,1,0:T(8,128)} %get-tuple-element.6, f32[32]{0:T(128)S(1)} %get-tuple-element.9), kind=kLoop, calls=%fused_computation | loop fusion | flops 2359296 | bytes 11796736 | tf_op jit(solution)/shard_map/add | solution.py:455
  50.4 0.0 copy-done.1
Async XLA Ops:
  2.7 42.0 %copy-start = (f32[1,6,32,3072]{3,2,1,0:T(8,128)S(1)}, f32[1,6,32,3072]{3,2,1,0:T(8,128)}, u32[]{:S(2)}) copy-start(f32[1,6,32,3072]{3,2,1,0:T(8,128)} %dir_h.1) | copy-start | bytes 7077892
  44.7 5.6 %copy-start.1 = (f32[32]{0:T(128)}, f32[32]{0:T(128)S(1)}, u32[]{:S(2)}) copy-start(f32[32]{0:T(128)S(1)} %get-tuple-element.9) | copy-start | bytes 388

commit v2 on v1

--- a/solution.py
+++ b/solution.py
@@ -58,8 +58,9 @@
     in_sem, s1, r1, s2, r2, s3, r3, own_sem, out_sem,
 ):
     me = lax.axis_index("dev")
-    rows = 4 * slots
-    total_rows = rows * nd
+    groups = slots // 2
+    half = 8 * nd
+    total_rows = half * groups
     order_rows = 2 * nd
     cs = 3 * sims
 
@@ -92,7 +93,8 @@
     def build_e(c, carry):
         r0 = c * 128
         row = iota((128, K), 0) + r0
-        pick = (row // 4 == iota((128, K), 1)).astype(F32).astype(BF16)
+        cycle = (row // 8) % nd * slots + row // half * 2 + (row // 4) % 2
+        pick = (cycle == iota((128, K), 1)).astype(F32).astype(BF16)
         block = dot_nt(pick, onehot_t)
         for oh in range(4):
             E[pl.ds(pl.multiple_of(r0, 128), 128), oh * K : (oh + 1) * K] = jnp.where(
@@ -153,60 +155,58 @@
                     live, block, 0.0
                 ).astype(BF16)
 
-    CH = min(512, total_rows)
-
-    def fill1(c, carry):
-        at = pl.ds(pl.multiple_of(c * CH, CH), CH)
-        send1[at, :] = dot_nt(E[at, :], F[...]).astype(BF16)
-        return carry
-
-    lax.fori_loop(0, total_rows // CH, fill1, 0)
-
-    pl.semaphore_wait(barrier, nd - 1)
-
-    def block_at(ref, d, size):
-        return ref.at[pl.ds(pl.multiple_of(d * size, size), size)]
-
-    def remote(send, recv, ss, rs, i, size):
+    def pack(x):
+        parts = [x[:, 0:128].reshape(nd, 8, 128), x[:, 128:256].reshape(nd, 8, 128)]
+        return jnp.concatenate(parts, axis=1).astype(BF16)
+
+    def unpack(x):
+        x = x.astype(F32)
+        parts = [x[:, 0:8].reshape(half, 128), x[:, 8:16].reshape(half, 128)]
+        return jnp.concatenate(parts, axis=1)
+
+    def remote(send, recv, ss, rs, g, i):
         dst = lax.rem(me + i, nd)
         return pltpu.make_async_remote_copy(
-            src_ref=send if size is None else block_at(send, dst, size),
-            dst_ref=recv.at[me] if size is None else block_at(recv, me, size),
-            send_sem=ss.at[i],
-            recv_sem=rs.at[i],
+            src_ref=send if g is None else send.at[g, dst],
+            dst_ref=recv.at[me] if g is None else recv.at[g, me],
+            send_sem=ss.at[i] if g is None else ss.at[g, i],
+            recv_sem=rs.at[i] if g is None else rs.at[g, i],
             device_id=(dst,),
             device_id_type=MESH,
         )
 
     def start_all(*args):
         def go(i, carry):
-            remote(*args[:4], i, args[4]).start()
+            remote(*args, i).start()
             return carry
 
         lax.fori_loop(1, nd, go, 0)
 
     def wait_recv_all(*args):
         def go(i, carry):
-            remote(*args[:4], i, args[4]).wait_recv()
+            remote(*args, i).wait_recv()
             return carry
 
         lax.fori_loop(1, nd, go, 0)
 
     def wait_send_all(*args):
         def go(i, carry):
-            remote(*args[:4], i, args[4]).wait_send()
+            remote(*args, i).wait_send()
             return carry
 
         lax.fori_loop(1, nd, go, 0)
 
-    def own(send, recv, i):
-        return pltpu.make_async_copy(
-            block_at(send, me, rows), block_at(recv, me, rows), own_sem.at[i]
-        )
-
-    ex1 = (send1, recv1, s1, r1, rows)
-    start_all(*ex1)
-    own(send1, recv1, 0).start()
+    def own(send, recv, e, g):
+        return pltpu.make_async_copy(send.at[g, me], recv.at[g, me], own_sem.at[e, g])
+
+    ex1 = (send1, recv1, s1, r1)
+    ex2 = (send2, recv2, s2, r2)
+    for g in range(groups):
+        send1[g] = pack(dot_nt(E[g * half : (g + 1) * half, :], F[...]))
+        if g == 0:
+            pl.semaphore_wait(barrier, nd - 1)
+        start_all(*ex1, g)
+        own(send1, recv1, 0, g).start()
 
     ids = ids_ref[...].astype(F32)
     OB = min(64, order_rows)
@@ -237,39 +237,9 @@
     odd = dot(jnp.broadcast_to((ids_ref[...] % 2).astype(F32), (8, nd)), spread)[0:1]
     g_row = jnp.where((odd > 0.5) & (lane % 2 == 1), -1.0, 1.0)
 
-    pr = prior_ref[...]
-    sigma = jnp.maximum(jnp.max(jnp.abs(pr)), 1.0)
-    pr8 = jnp.concatenate([pr, pr], axis=0)
-    rolled = pltpu.roll(pr8, L - my_m, 1)
-    first_row = iota((8, L), 1) < L - my_m
-    prior[...] = jnp.where(first_row, rolled, pr8)
-    inv_sigma = 1.0 / jnp.full((sims, 128), sigma, F32)
-
     loads[4].wait()
-    loads[5].wait()
-
-    def fold(x):
-        x = x[0] + x[1] + x[2] + x[3] + x[4] + x[5]
-        out = x[:, 0:128]
-        for i in range(1, x.shape[1] // 128):
-            out = out + x[:, i * 128 : (i + 1) * 128]
-        return out
-
-    norm = jnp.zeros((sims, 128), F32)
-    for c in range(L // JC):
-        x = res[:, :, c * JC : (c + 1) * JC]
-        norm = norm + fold(x * x)
-    accs[0:sims, :] = norm
-    accs[sims : 4 * sims, :] = jnp.zeros((3 * sims, 128), F32)
-
-    own(send1, recv1, 0).wait()
-    wait_recv_all(*ex1)
-
-    def slot(tl, carry):
-        a = iota((2 * order_rows, total_rows), 0)
-        want = ((a // 2) % nd) * rows + tl * 4 + (a % 2) * 2 + a // order_rows
-        sel = (iota((2 * order_rows, total_rows), 1) == want).astype(F32).astype(BF16)
-        D = dot(sel, recv1[...])
+
+    def slot(tl, D):
         mt = jnp.concatenate(
             [
                 jnp.concatenate([D[0:order_rows, 0:128], D[order_rows:, 0:128]], axis=1),
@@ -283,40 +253,69 @@
         for c in range(pix // PC):
             at = slice(c * PC, (c + 1) * PC)
             sky = dot(M, basis[tl, :, at]).reshape(2, 3, sims, PC)
-            inside = iota((2, 3, PC), 2) + c * PC < n
+            inside = iota((3, 2, PC), 2) + c * PC < n
             wt = jnp.where(inside, nw[tl, :, :, at], 0.0)
-            weighted[:, at] = (sky * wt[:, :, None, :]).reshape(2 * cs, PC).astype(BF16)
+            for h in range(2):
+                part = sky[h] * wt[:, h : h + 1, :]
+                weighted[h * cs : (h + 1) * cs, at] = part.reshape(cs, PC).astype(BF16)
         back = dot_nt(weighted[...], basis[tl])
         north = back[0:cs]
         south = back[cs : 2 * cs] * g_row
         pad = jnp.zeros((128 - cs, 2 * order_rows), F32)
         for q, par in enumerate((north + south, north - south)):
             pt = jnp.concatenate([par, pad], axis=0).T.astype(BF16)
-            at = pl.ds(pl.multiple_of((tl * 2 + q) * order_rows, order_rows), order_rows)
-            PAR[at, 0:128] = pt[0:order_rows]
-            PAR[at, 128:256] = pt[order_rows:]
-        return carry
-
-    lax.fori_loop(0, slots, slot, 0)
-
-    def fill2(c, carry):
-        at = pl.ds(pl.multiple_of(c * CH, CH), CH)
-        b = iota((CH, total_rows), 0) + c * CH
-        want = ((((b // 4) % slots) * 2 + b % 2) * nd + b // rows) * 2 + (b // 2) % 2
-        sel = (iota((CH, total_rows), 1) == want).astype(F32).astype(BF16)
-        send2[at, :] = dot(sel, PAR[...]).astype(BF16)
-        return carry
-
-    lax.fori_loop(0, total_rows // CH, fill2, 0)
-
-    ex2 = (send2, recv2, s2, r2, rows)
-    start_all(*ex2)
-    own(send2, recv2, 1).start()
-    wait_send_all(*ex1)
-    own(send2, recv2, 1).wait()
-    wait_recv_all(*ex2)
-
-    GT = dot(recv2[...].astype(F32).T.astype(BF16), E[...])
+            r0 = ((tl % 2) * 2 + q) * order_rows
+            PAR[r0 : r0 + order_rows, 0:128] = pt[0:order_rows]
+            PAR[r0 : r0 + order_rows, 128:256] = pt[order_rows:]
+
+    a = iota((half, half), 0)
+    want = (a // 2) % nd * 8 + a // (4 * nd) * 4 + a % 2 * 2 + a // (2 * nd) % 2
+    gather = (iota((half, half), 1) == want).astype(F32).astype(BF16)
+    want = ((a // 4 % 2 * 2 + a % 2) * nd + a // 8) * 2 + a // 2 % 2
+    scatter = (iota((half, half), 1) == want).astype(F32).astype(BF16)
+    for g in range(groups):
+        own(send1, recv1, 0, g).wait()
+        wait_recv_all(*ex1, g)
+        D = dot(gather, unpack(recv1[g]).astype(BF16))
+        for i in range(2):
+            slot(2 * g + i, D[2 * i * order_rows : 2 * (i + 1) * order_rows])
+        send2[g] = pack(dot(scatter, PAR[...]))
+        start_all(*ex2, g)
+        own(send2, recv2, 1, g).start()
+
+    pr = prior_ref[...]
+    sigma = jnp.maximum(jnp.max(jnp.abs(pr)), 1.0)
+    pr8 = jnp.concatenate([pr, pr], axis=0)
+    rolled = pltpu.roll(pr8, L - my_m, 1)
+    first_row = iota((8, L), 1) < L - my_m
+    prior[...] = jnp.where(first_row, rolled, pr8)
+    inv_sigma = 1.0 / jnp.full((sims, 128), sigma, F32)
+
+    loads[5].wait()
+
+    def fold(x):
+        x = x[0] + x[1] + x[2] + x[3] + x[4] + x[5]
+        out = x[:, 0:128]
+        for i in range(1, x.shape[1] // 128):
+            out = out + x[:, i * 128 : (i + 1) * 128]
+        return out
+
+    norm = jnp.zeros((sims, 128), F32)
+    for c in range(L // JC):
+        x = res[:, :, c * JC : (c + 1) * JC]
+        norm = norm + fold(x * x)
+    accs[0:sims, :] = norm
+    accs[sims : 4 * sims, :] = jnp.zeros((3 * sims, 128), F32)
+
+    for g in range(groups):
+        wait_send_all(*ex1, g)
+
+    GT = None
+    for g in range(groups):
+        own(send2, recv2, 1, g).wait()
+        wait_recv_all(*ex2, g)
+        add = dot(unpack(recv2[g]).T.astype(BF16), E[g * half : (g + 1) * half, :])
+        GT = add if GT is None else GT + add
     for s in range(2):
         live = alive(s, 256)
         G = [
@@ -377,14 +376,26 @@
     start_all(*ex3)
     for out in outs:
         out.wait()
-    wait_send_all(*ex2)
+    for g in range(groups):
+        wait_send_all(*ex2, g)
     wait_recv_all(*ex3)
     total = precv[0]
     for i in range(1, nd):
         total = total + precv[i]
-    stats_ref[0:8, :] = total
-    stats_ref[8:16, :] = jnp.full((8, 4 * sims), sigma, F32)
+    stats_ref[0 : 4 * sims, :] = jnp.broadcast_to(total.T[:, 0:1], (4 * sims, 128))
+    stats_ref[4 * sims : 5 * sims, :] = jnp.full((sims, 128), sigma, F32)
     wait_send_all(*ex3)
+
+
+def update(sims, stats, res, drn, img, res_out, dir_out, step_out):
+    norm_old, da, ra, aa, sigma = [stats[i * sims : (i + 1) * sims, :] for i in range(5)]
+    scaled = norm_old / da
+    step = scaled / sigma
+    ratio = (norm_old - 2.0 * scaled * ra + scaled * scaled * aa) / norm_old
+    step_out[...] = step.T[0:1, :]
+    after = res[0, 0] - step[:, 0:1] * img[0, 0]
+    res_out[0, 0] = after
+    dir_out[0, 0] = after + ratio[:, 0:1] * drn[0, 0]
 
 
 def body(
@@ -396,8 +407,10 @@
     slots = cycle_length.shape[0]
     pix = noise_weight.shape[3]
     assert direction.shape[0] == 1
-    rows = 4 * slots
-    total_rows = rows * nd
+    assert slots % 2 == 0
+    groups = slots // 2
+    half = 8 * nd
+    total_rows = half * groups
     vmem = pl.BlockSpec(memory_space=pltpu.VMEM)
     smem = pl.BlockSpec(memory_space=pltpu.SMEM)
     hbm = pl.BlockSpec(memory_space=pl.ANY)
@@ -406,7 +419,7 @@
         functools.partial(kernel, nd, slots, K, sims, pix),
         out_shape=(
             jax.ShapeDtypeStruct(direction.shape, F32),
-            jax.ShapeDtypeStruct((16, 4 * sims), F32),
+            jax.ShapeDtypeStruct((5 * sims, 128), F32),
         ),
         in_specs=[hbm] * 6 + [vmem] * 3 + [smem] * 4,
         out_specs=(hbm, vmem),
@@ -415,18 +428,18 @@
             pltpu.VMEM((6, sims, L), F32),
             pltpu.VMEM((L, K), BF16),
             pltpu.VMEM((L, 2 * K), BF16),
-            pltpu.VMEM((slots, 2, 3, pix), F32),
+            pltpu.VMEM((slots, 3, 2, pix), F32),
             pltpu.VMEM((total_rows, 4 * K), BF16),
             pltpu.VMEM((8 * sims, K), F32),
             pltpu.VMEM((16 * sims, 2 * K), F32),
             pltpu.VMEM((256, 4 * K), BF16),
-            pltpu.VMEM((total_rows, 256), BF16),
-            pltpu.VMEM((total_rows, 256), BF16),
-            pltpu.VMEM((total_rows, 256), BF16),
-            pltpu.VMEM((total_rows, 256), BF16),
+            pltpu.VMEM((groups, nd, 16, 128), BF16),
+            pltpu.VMEM((groups, nd, 16, 128), BF16),
+            pltpu.VMEM((groups, nd, 16, 128), BF16),
+            pltpu.VMEM((groups, nd, 16, 128), BF16),
             pltpu.VMEM((slots, 4 * nd, pix), BF16),
             pltpu.VMEM((6 * sims, pix), BF16),
-            pltpu.VMEM((total_rows, 256), BF16),
+            pltpu.VMEM((half, 256), BF16),
             pltpu.VMEM((8 * sims, K), BF16),
             pltpu.VMEM((16 * sims, 2 * K), BF16),
             pltpu.VMEM((8, L), F32),
@@ -434,25 +447,33 @@
             pltpu.VMEM((4 * sims, 128), F32),
             pltpu.VMEM((8, 4 * sims), F32),
             pltpu.VMEM((nd, 8, 4 * sims), F32),
-            dma((6,)), dma((nd,)), dma((nd,)), dma((nd,)), dma((nd,)), dma((nd,)), dma((nd,)),
-            dma((2,)), dma((L // JC,)),
+            dma((6,)), *[dma((groups, nd))] * 4, dma((nd,)), dma((nd,)),
+            dma((2, groups)), dma((L // JC,)),
         ],
         compiler_params=pltpu.CompilerParams(
             collective_id=0, has_side_effects=True, vmem_limit_bytes=60 * 1024 * 1024
         ),
         name="cg",
     )(
-        residual, direction, legendre_scalar, legendre_plus, legendre_minus, noise_weight,
-        prior_inverse, order_ids.reshape(1, -1), cycle_assign.reshape(1, -1),
+        residual, direction, legendre_scalar, legendre_plus, legendre_minus,
+        jnp.transpose(noise_weight, (0, 2, 1, 3)), prior_inverse, order_ids.reshape(1, -1), cycle_assign.reshape(1, -1),
         order_ids, live_blocks, cycle_length, cycle_shift,
     )
-    norm_old, da, ra, aa = [stats[0, i * sims : (i + 1) * sims] for i in range(4)]
-    scaled_step = norm_old / da
-    step_length = scaled_step / stats[8, 0:sims]
-    norm_new = norm_old - 2.0 * scaled_step * ra + scaled_step * scaled_step * aa
-    ratio = norm_new / norm_old
-    residual_next = residual - step_length[None, None, :, None] * image
-    direction_next = residual_next + ratio[None, None, :, None] * direction
+    block = pl.BlockSpec((1, 1, sims, L), lambda i: (0, i, 0, 0))
+    residual_next, direction_next, step = pl.pallas_call(
+        functools.partial(update, sims),
+        grid=(6,),
+        out_shape=(
+            jax.ShapeDtypeStruct(direction.shape, F32),
+            jax.ShapeDtypeStruct(direction.shape, F32),
+            jax.ShapeDtypeStruct((1, sims), F32),
+        ),
+        in_specs=[pl.BlockSpec((5 * sims, 128), lambda i: (0, 0)), block, block, block],
+        out_specs=(block, block, pl.BlockSpec((1, sims), lambda i: (0, 0))),
+        compiler_params=pltpu.CompilerParams(vmem_limit_bytes=60 * 1024 * 1024),
+        name="update",
+    )(stats, residual, direction, image)
+    step_length = step.reshape(-1)
     return (residual_next, direction_next, step_length)
 
 

time: 50.6 us -> 46.5 us (0.919)
  other arithmetic: 6.54 us -> 0 us
  Pallas kernels: 41.1 us -> 45.6 us
  local copies, waits for them, and re-layouts: 2.07 us -> 0 us
    pallas_call x0 -> x1, Pallas kernels: none -> 6.86 us  [body(): pl.pallas_call(functools.partial(update, sims), grid=(6,), out_shape=(jax...]
    add x1 -> x0, other arithmetic: 5.63 us -> none  [body(): direction_next = residual_next + ratio[None, None, :, None] * direction]
    pallas_call x1, Pallas kernels: 41.1 us -> 38.7 us  [body(): pl.pallas_call(functools.partial(kernel, nd, slots, K, sims, pix), out_sh...]
    unnamed x5 -> x0, local copies, waits for them, and re-layouts: 2.07 us -> none
    div x1 -> x0, other arithmetic: 0.91 us -> none  [body(): step_length = scaled_step / stats[8, 0:sims]]
where the time goes in v2:
time: 46.5 us; the launch traced here: 46.2 us
  Pallas kernels  45.6 us (98%)
  between operations  0.64 us (1%)
    pallas_call x1, Pallas kernels, body(): pl.pallas_call(functools.partial(kernel, nd, slots, K, sims, pix), out_sh...  38.7 us
    pallas_call x1, Pallas kernels, body(): pl.pallas_call(functools.partial(update, sims), grid=(6,), out_shape=(jax...  6.86 us

profile of v2, /device:TPU:0, one launch (start us, length us, event | category | flops | bytes accessed | tf_op | source)
XLA Modules:
  0.0 46.2 jit_solution(6813016572958340957)
XLA Ops:
  0.6 38.7 %cg.1 = (f32[1,6,32,3072]{3,2,1,0:T(8,128)}, f32[160,128]{1,0:T(8,128)}) custom-call(f32[1,6,32,3072]{3,2,1,0:T(8,128)} %res.1, f32[1,6,32,3072]{3,2,1,0:T(8,128)} %drn.1, bf16[1,3072,128]{2,1,0:T(8,128)(2,1)} %ts_h.1, bf16[1,3072,128]{2,1,0:T(8,128)(2,1)} %tp_h.1, bf16[1,3072,128]{2,1,0:T(8,128)(2,1)} %tm_h.1, f32[4,3,2,4096]{3,2,1,0:T(2,128)} %bitcast.4, ...), custom_call_target="tpu_custom_call" | custom-call | tf_op jit(solution)/shard_map/cg/pallas_call | solution.py:418
  39.3 6.9 %update.1 = (f32[1,6,32,3072]{3,2,1,0:T(8,128)}, f32[1,6,32,3072]{3,2,1,0:T(8,128)}, f32[1,32]{1,0:T(1,128)}) custom-call(f32[160,128]{1,0:T(8,128)} %get-tuple-element.8.stats, f32[1,6,32,3072]{3,2,1,0:T(8,128)} %res.1, f32[1,6,32,3072]{3,2,1,0:T(8,128)} %drn.1, f32[1,6,32,3072]{3,2,1,0:T(8,128)} %get-tuple-element.9.img), custom_call_target="tpu_custom_call" | custom-call | tf_op jit(solution)/shard_map/update/pallas_call | solution.py:463

commit v3 on v2

--- a/solution.py
+++ b/solution.py
@@ -10,6 +10,7 @@
 L = 3072
 BLOCKS = 4
 JC = 512
+FC = 1024
 PC = 512
 F32 = jnp.float32
 BF16 = jnp.bfloat16
@@ -107,21 +108,21 @@
     for load in loads[:4]:
         load.wait()
 
-    def lane_masks(j0):
-        lane = iota((1, JC), 1) + j0
+    def lane_masks(j0, size=JC):
+        lane = iota((1, size), 1) + j0
         return lane < L - my_m, lane % 2 == 0
 
-    for c in range(L // JC):
-        first, even = lane_masks(c * JC)
+    for c in range(L // FC):
+        first, even = lane_masks(c * FC, FC)
         alt = jnp.where(even, 1.0, -1.0)
         m0 = first.astype(F32)
         m1 = 1.0 - m0
-        x = drn[:, :, c * JC : (c + 1) * JC].reshape(6 * sims, JC)
+        x = drn[:, :, c * FC : (c + 1) * FC].reshape(6 * sims, FC)
         parts = [(x * m).astype(BF16) for m in (m0, m0 * alt, m1, m1 * alt)]
         lhs_t = jnp.concatenate([p[: 2 * sims] for p in parts], axis=0)
         lhs_eb = jnp.concatenate([p[2 * sims :] for p in parts], axis=0)
-        add_t = dot(lhs_t, ts[c * JC : (c + 1) * JC, :])
-        add_eb = dot(lhs_eb, teb[c * JC : (c + 1) * JC, :])
+        add_t = dot(lhs_t, ts[c * FC : (c + 1) * FC, :])
+        add_eb = dot(lhs_eb, teb[c * FC : (c + 1) * FC, :])
         if c == 0:
             acc_t[...] = add_t
             acc_eb[...] = add_eb
@@ -232,10 +233,13 @@
 
             lax.fori_loop(0, pix // 128, step, (2.0 * co, -2.0 * si))
 
-    lane = iota((1, 2 * order_rows), 1)
-    spread = (iota((nd, 2 * order_rows), 0) == (lane % order_rows) // 2).astype(F32)
-    odd = dot(jnp.broadcast_to((ids_ref[...] % 2).astype(F32), (8, nd)), spread)[0:1]
-    g_row = jnp.where((odd > 0.5) & (lane % 2 == 1), -1.0, 1.0)
+    row = iota((2 * order_rows, nd), 0)
+    odd = jnp.where(iota((2 * order_rows, nd), 1) == row % order_rows // 2, ids_ref[...] % 2, 0)
+    odd = jnp.sum(odd.astype(F32), axis=1, keepdims=True)
+    flips = (odd > 0.5) & (iota((2 * order_rows, 1), 0) % 2 == 1)
+    g_col = jnp.where(flips, -1.0, 1.0)
+    for h in range(2):
+        weighted[h * 128 + cs : (h + 1) * 128, :] = jnp.zeros((128 - cs, pix), BF16)
 
     loads[4].wait()
 
@@ -257,13 +261,12 @@
             wt = jnp.where(inside, nw[tl, :, :, at], 0.0)
             for h in range(2):
                 part = sky[h] * wt[:, h : h + 1, :]
-                weighted[h * cs : (h + 1) * cs, at] = part.reshape(cs, PC).astype(BF16)
-        back = dot_nt(weighted[...], basis[tl])
-        north = back[0:cs]
-        south = back[cs : 2 * cs] * g_row
-        pad = jnp.zeros((128 - cs, 2 * order_rows), F32)
+                weighted[h * 128 : h * 128 + cs, at] = part.reshape(cs, PC).astype(BF16)
+        back = dot_nt(basis[tl], weighted[...])
+        north = back[:, 0:128]
+        south = back[:, 128:256] * g_col
         for q, par in enumerate((north + south, north - south)):
-            pt = jnp.concatenate([par, pad], axis=0).T.astype(BF16)
+            pt = par.astype(BF16)
             r0 = ((tl % 2) * 2 + q) * order_rows
             PAR[r0 : r0 + order_rows, 0:128] = pt[0:order_rows]
             PAR[r0 : r0 + order_rows, 128:256] = pt[order_rows:]
@@ -387,15 +390,34 @@
     wait_send_all(*ex3)
 
 
-def update(sims, stats, res, drn, img, res_out, dir_out, step_out):
+def update(
+    sims, stats, res_h, drn_h, img_h, res_out, dir_out, step_out, res, drn, img, in_sem, out_sem
+):
+    loads = []
+    for c in range(6):
+        triple = [(res_h, res), (drn_h, drn), (img_h, img)]
+        for k, (src, dst) in enumerate(triple):
+            load = pltpu.make_async_copy(src.at[0, c], dst.at[c], in_sem.at[k, c])
+            load.start()
+            loads.append(load)
     norm_old, da, ra, aa, sigma = [stats[i * sims : (i + 1) * sims, :] for i in range(5)]
     scaled = norm_old / da
     step = scaled / sigma
     ratio = (norm_old - 2.0 * scaled * ra + scaled * scaled * aa) / norm_old
     step_out[...] = step.T[0:1, :]
-    after = res[0, 0] - step[:, 0:1] * img[0, 0]
-    res_out[0, 0] = after
-    dir_out[0, 0] = after + ratio[:, 0:1] * drn[0, 0]
+    stores = []
+    for c in range(6):
+        for load in loads[3 * c : 3 * c + 3]:
+            load.wait()
+        after = res[c] - step[:, 0:1] * img[c]
+        res[c] = after
+        drn[c] = after + ratio[:, 0:1] * drn[c]
+        for k, (src, dst) in enumerate([(res, res_out), (drn, dir_out)]):
+            store = pltpu.make_async_copy(src.at[c], dst.at[0, c], out_sem.at[k, c])
+            store.start()
+            stores.append(store)
+    for store in stores:
+        store.wait()
 
 
 def body(
@@ -438,7 +460,7 @@
             pltpu.VMEM((groups, nd, 16, 128), BF16),
             pltpu.VMEM((groups, nd, 16, 128), BF16),
             pltpu.VMEM((slots, 4 * nd, pix), BF16),
-            pltpu.VMEM((6 * sims, pix), BF16),
+            pltpu.VMEM((256, pix), BF16),
             pltpu.VMEM((half, 256), BF16),
             pltpu.VMEM((8 * sims, K), BF16),
             pltpu.VMEM((16 * sims, 2 * K), BF16),
@@ -459,17 +481,16 @@
         jnp.transpose(noise_weight, (0, 2, 1, 3)), prior_inverse, order_ids.reshape(1, -1), cycle_assign.reshape(1, -1),
         order_ids, live_blocks, cycle_length, cycle_shift,
     )
-    block = pl.BlockSpec((1, 1, sims, L), lambda i: (0, i, 0, 0))
     residual_next, direction_next, step = pl.pallas_call(
         functools.partial(update, sims),
-        grid=(6,),
         out_shape=(
             jax.ShapeDtypeStruct(direction.shape, F32),
             jax.ShapeDtypeStruct(direction.shape, F32),
             jax.ShapeDtypeStruct((1, sims), F32),
         ),
-        in_specs=[pl.BlockSpec((5 * sims, 128), lambda i: (0, 0)), block, block, block],
-        out_specs=(block, block, pl.BlockSpec((1, sims), lambda i: (0, 0))),
+        in_specs=[vmem, hbm, hbm, hbm],
+        out_specs=(hbm, hbm, vmem),
+        scratch_shapes=[pltpu.VMEM((6, sims, L), F32)] * 3 + [dma((3, 6)), dma((2, 6))],
         compiler_params=pltpu.CompilerParams(vmem_limit_bytes=60 * 1024 * 1024),
         name="update",
     )(stats, residual, direction, image)

time: 46.5 us -> 46.7 us (level)
  no operation moved by 1% of the time
where the time goes in v3:
time: 46.7 us; the launch traced here: 46.5 us
  Pallas kernels  45.9 us (98%)
  between operations  0.64 us (1%)
    pallas_call x1, Pallas kernels, body(): pl.pallas_call(functools.partial(kernel, nd, slots, K, sims, pix), out_sh...  39.2 us
    pallas_call x1, Pallas kernels, body(): pl.pallas_call(functools.partial(update, sims), out_shape=(jax.ShapeDtype...  6.71 us

profile of v3, /device:TPU:0, one launch (start us, length us, event | category | flops | bytes accessed | tf_op | source)
XLA Modules:
  0.0 46.5 jit_solution(16006633272955622444)
XLA Ops:
  0.6 39.2 %cg.1 = (f32[1,6,32,3072]{3,2,1,0:T(8,128)}, f32[160,128]{1,0:T(8,128)}) custom-call(f32[1,6,32,3072]{3,2,1,0:T(8,128)} %res_h.3, f32[1,6,32,3072]{3,2,1,0:T(8,128)} %drn_h.1, bf16[1,3072,128]{2,1,0:T(8,128)(2,1)} %ts_h.1, bf16[1,3072,128]{2,1,0:T(8,128)(2,1)} %tp_h.1, bf16[1,3072,128]{2,1,0:T(8,128)(2,1)} %tm_h.1, f32[4,3,2,4096]{3,2,1,0:T(2,128)} %bitcast.4, ...), custom_call_target="tpu_custom_call" | custom-call | tf_op jit(solution)/shard_map/cg/pallas_call | solution.py:440
  39.8 6.7 %update.1 = (f32[1,6,32,3072]{3,2,1,0:T(8,128)}, f32[1,6,32,3072]{3,2,1,0:T(8,128)}, f32[1,32]{1,0:T(1,128)}) custom-call(f32[160,128]{1,0:T(8,128)} %get-tuple-element.8.stats, f32[1,6,32,3072]{3,2,1,0:T(8,128)} %res_h.3, f32[1,6,32,3072]{3,2,1,0:T(8,128)} %drn_h.1, f32[1,6,32,3072]{3,2,1,0:T(8,128)} %get-tuple-element.9.img_h), custom_call_target="tpu_custom_call" | custom-call | tf_op jit(solution)/shard_map/update/pallas_call | solution.py:484
